TPU v7x, 1024 devices: a whole 8x8x8 slice. The times are simulated.
1024 devices in a mesh: ep: 16 (over z, core), rep: 8 (over y), opt: 8 (over x).
Axes of the slice: x: 8, y: 8, z: 8, core: 2. Of those that a mesh axis runs over, the one named last changes fastest.
Arguments:
- incoming_tokens: bfloat16 [16, 8, 8, 128, 2048], P('ep', 'rep', None, None, 'opt'), may hold values from -6 to 6
- cotangent: bfloat16 [16, 8, 8, 128, 2048], P('ep', 'rep', None, None, 'opt'), may hold values from -6 to 6
- block_dest: int32 [16, 8, 8], replicated, may hold values from 0 to 15, as said below
- gate_weight: bfloat16 [16, 2048, 768], P('ep'), may hold values from -0.125 to 0.125
- up_weight: bfloat16 [16, 2048, 768], P('ep'), may hold values from -0.125 to 0.125
- basis: bfloat16 [16, 768, 512], P('ep'), may hold values from -0.21875 to 0.21875
- moment_first: float32 [16, 512, 2048], P('ep', 'rep', 'opt'), may hold values from -6 to 6
- moment_second: float32 [16, 512, 2048], P('ep', 'rep', 'opt'), may hold values from 0.05 to 1
Outputs:
- first_moment: float32 [16, 512, 2048], P('ep', 'rep', 'opt')
- second_moment: float32 [16, 512, 2048], P('ep', 'rep', 'opt')
- weight_delta: bfloat16 [16, 768, 2048], P('ep', None, 'opt')
Inputs may be any that keep to these rules, and one draw needn't show every extreme that they name: `block_dest`: the 8 blocks of one pair of indices (s, r) go to 8 different instances.
All inputs are finite; a program needn't handle non-finite values.
Results may differ from a plain program's by a relative error of at most 0.0085.
Values may be sent and summed in bfloat16 or wider, within the bound.
A program may use at most 32 MiB of HBM per device.

v0:
```python
import jax
import jax.numpy as jnp
from jax import lax
from jax.sharding import PartitionSpec as P

beta_one = 0.9
beta_two = 0.999
adam_step = 1000.0
adam_eps = 1e-08


def project_slots(slot_rows, slot_flags, gate_matrix, up_matrix, projector_matrix):

    def compute_block(block_rows):
        gate_values = jnp.dot(block_rows, gate_matrix, preferred_element_type=jnp.float32)
        up_values = jnp.dot(block_rows, up_matrix, preferred_element_type=jnp.float32)
        hidden = (jax.nn.silu(gate_values) * up_values).astype(jnp.bfloat16)
        return jnp.dot(hidden, projector_matrix, preferred_element_type=jnp.float32).astype(
            jnp.bfloat16
        )

    def empty_block(block_rows):
        return jnp.zeros((block_rows.shape[0], projector_matrix.shape[1]), jnp.bfloat16)

    pieces = [
        lax.cond(slot_flags[position], compute_block, empty_block, slot_rows[position])
        for position in range(slot_rows.shape[0])
    ]
    return jnp.concatenate(pieces, axis=0)


def shards(
    incoming_tokens,
    cotangent,
    block_dest,
    gate_weight,
    up_weight,
    basis,
    moment_first,
    moment_second,
):
    expert_parallel_index = lax.axis_index("ep")
    rep_index = lax.axis_index("rep")
    opt_index = lax.axis_index("opt")
    ep_count = lax.axis_size("ep")
    opt_count = lax.axis_size("opt")
    per_device = ep_count // opt_count
    rep_plane = lax.dynamic_index_in_dim(block_dest, rep_index, 1, keepdims=False)
    own_dest = lax.dynamic_index_in_dim(rep_plane, expert_parallel_index, 0, keepdims=False)
    choose_branch = (own_dest[None, :] == jnp.arange(ep_count, dtype=jnp.int32)[:, None]).astype(
        jnp.bfloat16
    )
    token_slots = jnp.einsum(
        "mc,cuy->muy", choose_branch, incoming_tokens[0, 0], preferred_element_type=jnp.float32
    ).astype(jnp.bfloat16)
    cotangent_slots = jnp.einsum(
        "mc,cuy->muy", choose_branch, cotangent[0, 0], preferred_element_type=jnp.float32
    ).astype(jnp.bfloat16)
    arrivals = jnp.any(rep_plane == expert_parallel_index, axis=1)
    slot_flags = lax.dynamic_slice_in_dim(arrivals, opt_index * per_device, per_device)
    gate_matrix = gate_weight[0]
    up_matrix = up_weight[0]
    projector_matrix = basis[0]
    token_rows, upstream_gradient_rows = (
        lax.all_to_all(
            lax.all_to_all(token_slots, "ep", split_axis=0, concat_axis=0, tiled=True),
            "opt",
            split_axis=0,
            concat_axis=2,
            tiled=True,
        ),
        lax.all_to_all(
            lax.all_to_all(cotangent_slots, "ep", split_axis=0, concat_axis=0, tiled=True),
            "opt",
            split_axis=0,
            concat_axis=2,
            tiled=True,
        ),
    )
    projected = project_slots(token_rows, slot_flags, gate_matrix, up_matrix, projector_matrix)
    feature_width = upstream_gradient_rows.shape[2]
    partial_full = jnp.dot(
        projected.T,
        upstream_gradient_rows.reshape(-1, feature_width),
        preferred_element_type=jnp.float32,
    )
    partial_value = lax.psum_scatter(partial_full, "opt", scatter_dimension=1, tiled=True)
    gradient = lax.psum_scatter(partial_value, "rep", scatter_dimension=0, tiled=True)
    first_moment = beta_one * moment_first[0] + (1.0 - beta_one) * gradient
    second_moment = beta_two * moment_second[0] + (1.0 - beta_two) * gradient * gradient
    scaled_first = first_moment / (1.0 - beta_one**adam_step)
    scaled_second = second_moment / (1.0 - beta_two**adam_step)
    update = (-scaled_first / (jnp.sqrt(scaled_second) + adam_eps)).astype(jnp.bfloat16)
    zero_delta = jnp.zeros((projector_matrix.shape[0], update.shape[1]), jnp.float32)
    shard_piece = lax.all_gather(update, "rep", axis=0, tiled=True)
    columns = lax.slice_in_dim(projector_matrix, 0, shard_piece.shape[0], axis=1)
    weight_change = zero_delta + jnp.dot(columns, shard_piece, preferred_element_type=jnp.float32)
    return (first_moment[None], second_moment[None], weight_change.astype(jnp.bfloat16)[None])


def solution(mesh):
    in_specs = (
        P("ep", "rep", None, None, "opt"),
        P("ep", "rep", None, None, "opt"),
        P(),
        P("ep", None, None),
        P("ep", None, None),
        P("ep", None, None),
        P("ep", "rep", "opt"),
        P("ep", "rep", "opt"),
    )
    out_specs = (P("ep", "rep", "opt"), P("ep", "rep", "opt"), P("ep", None, "opt"))
    return jax.shard_map(shards, mesh=mesh, in_specs=in_specs, out_specs=out_specs, check_vma=False)
```

profile of v0, /device:TPU:2, one launch (start us, length us, event | category | flops | bytes accessed | tf_op | source)
XLA Modules:
  0.0 304.7 jit_solution(4375117938279061682)
XLA Ops:
  7.2 0.0 copy-start
  7.2 0.0 copy-start.3
  7.2 1.0 dynamic-slice_reduce_fusion
  8.2 0.1 copy-done
  8.2 0.6 convolution_convert_fusion.3
  8.8 1.3 copy.21
  10.1 16.8 %all-to-all-start = ((bf16[16,128,256]{2,1,0:T(8,128)(2,1)}), bf16[16,128,256]{2,1,0:T(8,128)(2,1)S(1)}, u32[]{:S(2)}, u32[]{:S(2)}) async-start(bf16[16,128,256]{2,1,0:T(8,128)(2,1)} %copy.21), calls=%async_computation | async-start | bytes 2097152 | tf_op jit(solution)/shard_map/all_to_all | solution.py:66
  26.9 0.0 copy-done.3
  26.9 0.6 convolution_convert_fusion.2
  27.5 0.3 copy.24
  27.8 25.7 %all-to-all-done = bf16[16,128,256]{2,1,0:T(8,128)(2,1)S(1)} async-done(((bf16[16,128,256]{2,1,0:T(8,128)(2,1)}), bf16[16,128,256]{2,1,0:T(8,128)(2,1)S(1)}, u32[]{:S(2)}, u32[]{:S(2)}) %all-to-all-start) | async-done | bytes 1048608 | tf_op jit(solution)/shard_map/all_to_all | solution.py:66
  53.6 31.9 %all_to_all.40 = bf16[16,128,256]{2,1,0:T(8,128)(2,1)} all-to-all(bf16[16,128,256]{2,1,0:T(8,128)(2,1)S(1)} %copy.24), channel_id=1, replica_groups=mesh['ep'=16,'rep'=8,'opt'=8] {'ep'}, dimensions={0} | all-to-all | bytes 2097152 | tf_op jit(solution)/shard_map/all_to_all | solution.py:73
  85.5 35.5 %all_to_all.41 = bf16[16,128,256]{2,1,0:T(8,128)(2,1)} all-to-all(bf16[16,128,256]{2,1,0:T(8,128)(2,1)S(1)} %all-to-all-done), channel_id=1, replica_groups=mesh['ep'=16,'rep'=8,'opt'=8] {'opt'}, dimensions={0} | all-to-all | bytes 2097152 | tf_op jit(solution)/shard_map/all_to_all | solution.py:65
  121.0 5.2 %all-to-all-start.3 = ((bf16[16,128,256]{2,1,0:T(8,128)(2,1)}), bf16[16,128,256]{2,1,0:T(8,128)(2,1)S(1)}, u32[]{:S(2)}, u32[]{:S(2)}) async-start(bf16[16,128,256]{2,1,0:T(8,128)(2,1)} %all_to_all.40), calls=%async_computation.3 | async-start | bytes 2097152 | tf_op jit(solution)/shard_map/all_to_all | solution.py:72
  126.2 0.0 reduce-scatter.3.cloned.1.call-start
  126.2 0.7 fusion.26
  126.9 0.1 dynamic_slice.12
  127.0 0.6 fusion.34
  128.9 1.8 copy.35
  130.7 23.4 %all-to-all-done.3 = bf16[16,128,256]{2,1,0:T(8,128)(2,1)S(1)} async-done(((bf16[16,128,256]{2,1,0:T(8,128)(2,1)}), bf16[16,128,256]{2,1,0:T(8,128)(2,1)S(1)}, u32[]{:S(2)}, u32[]{:S(2)}) %all-to-all-start.3) | async-done | bytes 1048608 | tf_op jit(solution)/shard_map/all_to_all | solution.py:72
  154.1 0.6 copy.25
  154.7 0.3 copy.29
  155.0 0.7 conditional.2
  155.0 0.7 broadcast.14
  155.7 3.6 %fusion.19 = f32[512,2048]{1,0:T(8,128)} fusion(bf16[256,2048]{1,0:T(8,128)(2,1)S(1)} %bitcast.68, bf16[128,512]{1,0:T(8,128)(2,1)S(1)} %get-tuple-element.52, bf16[128,512]{1,0:T(8,128)(2,1)} %get-tuple-element.51), kind=kOutput, calls=%fused_computation.27 | convolution fusion | flops 537395200 | bytes 5505024 | tf_op jit(solution)/shard_map/dot_general | solution.py:82
  159.3 0.0 copy-start.4
  159.3 0.0 copy-start.5
  159.3 0.0 copy-start.1
  159.3 0.0 reduce-scatter.3.cloned.1.call-update
  159.3 0.0 reduce-scatter.5.cloned.1.call-start
  159.4 64.0 %reduce-scatter.3.cloned.1.call-done = f32[512,256]{1,0:T(8,128)} async-done(((f32[512,2048]{1,0:T(8,128)}), f32[512,256]{1,0:T(8,128)}) %reduce-scatter.3.cloned.1.call-update) | async-done | bytes 524304 | tf_op jit(solution)/shard_map/reduce_scatter | solution.py:87
  223.3 0.0 reduce-scatter.5.cloned.1.call-update
  223.4 46.9 %reduce-scatter.5.cloned.1.call-done = f32[64,256]{1,0:T(8,128)} async-done(((f32[512,256]{1,0:T(8,128)}), f32[64,256]{1,0:T(8,128)}) %reduce-scatter.5.cloned.1.call-update) | async-done | bytes 65552 | tf_op jit(solution)/shard_map/reduce_scatter | solution.py:88
  270.2 0.0 copy-done.4
  270.2 0.0 copy-done.5
  270.2 1.5 divide_convert_fusion
  271.8 24.8 %all_gather.3 = bf16[512,256]{1,0:T(8,128)(2,1)S(1)} all-gather(bf16[64,256]{1,0:T(8,128)(2,1)S(1)} %get-tuple-element.46), channel_id=1, replica_groups=mesh['ep'=16,'rep'=8,'opt'=8] {'rep'}, dimensions={0}, use_global_device_ids=true | all-gather | bytes 294912 | tf_op jit(solution)/shard_map/all_gather | solution.py:95
  296.5 0.0 copy-done.1
  296.5 0.4 fusion.16
  297.0 0.9 copy.26
  (2 shorter events, 0.0 us)
Async XLA Ops:
  7.2 1.1 copy-start
  7.2 19.7 %copy-start.3 = (bf16[1,1,8,128,256]{4,3,2,1,0:T(8,128)(2,1)S(1)}, bf16[1,1,8,128,256]{4,3,2,1,0:T(8,128)(2,1)}, u32[]{:S(2)}) copy-start(bf16[1,1,8,128,256]{4,3,2,1,0:T(8,128)(2,1)} %param.13) | copy-start | bytes 1572868
  10.1 43.5 %all-to-all-start = ((bf16[16,128,256]{2,1,0:T(8,128)(2,1)}), bf16[16,128,256]{2,1,0:T(8,128)(2,1)S(1)}, u32[]{:S(2)}, u32[]{:S(2)}) async-start(bf16[16,128,256]{2,1,0:T(8,128)(2,1)} %copy.21), calls=%async_computation | async-start | bytes 2097152 | tf_op jit(solution)/shard_map/all_to_all | solution.py:66
  121.0 33.1 %all-to-all-start.3 = ((bf16[16,128,256]{2,1,0:T(8,128)(2,1)}), bf16[16,128,256]{2,1,0:T(8,128)(2,1)S(1)}, u32[]{:S(2)}, u32[]{:S(2)}) async-start(bf16[16,128,256]{2,1,0:T(8,128)(2,1)} %all_to_all.40), calls=%async_computation.3 | async-start | bytes 2097152 | tf_op jit(solution)/shard_map/all_to_all | solution.py:72
  126.2 97.1 %reduce-scatter.3.cloned.1.call-start = ((), (), s32[]{:S(2)}) async-start(), calls=%async_computation.6 | async-start | bytes 4718592 | tf_op jit(solution)/shard_map/reduce_scatter | solution.py:87
  159.3 111.0 %copy-start.4 = (f32[1,64,256]{2,1,0:T(8,128)S(1)}, f32[1,64,256]{2,1,0:T(8,128)}, u32[]{:S(2)}) copy-start(f32[1,64,256]{2,1,0:T(8,128)} %param.18) | copy-start | bytes 196612
  159.3 111.0 %copy-start.5 = (f32[1,64,256]{2,1,0:T(8,128)S(1)}, f32[1,64,256]{2,1,0:T(8,128)}, u32[]{:S(2)}) copy-start(f32[1,64,256]{2,1,0:T(8,128)} %param.19) | copy-start | bytes 196612
  159.3 137.3 %copy-start.1 = (bf16[1,768,512]{2,1,0:T(8,128)(2,1)S(1)}, bf16[1,768,512]{2,1,0:T(8,128)(2,1)}, u32[]{:S(2)}) copy-start(bf16[1,768,512]{2,1,0:T(8,128)(2,1)} %param.17) | copy-start | bytes 2359300
  159.3 110.9 %reduce-scatter.5.cloned.1.call-start = ((), (), s32[]{:S(2)}) async-start(), calls=%async_computation.7 | async-start | bytes 589824 | tf_op jit(solution)/shard_map/reduce_scatter | solution.py:88
Sparse Core Ops, SparseCore 0:
  159.4 63.8 reduce-scatter.2
  226.7 43.4 reduce-scatter.4
where the time goes:
time: 305 us
  waiting for transfers between devices  160 us (52%)
  blocking collectives  92.2 us (30%)
  starting transfers between devices  22 us (7%)
  between operations  15.4 us (5%)
  local copies, waits for them, and re-layouts  7.66 us (3%)
  matrix products  5.14 us (2%)
    reduce_scatter x1, waiting for transfers between devices, shards(): lax.psum_scatter(partial_full, 'opt', scatter_dimension=1, tiled=True)  64 us
    reduce_scatter x1, waiting for transfers between devices, shards(): lax.psum_scatter(partial_value, 'rep', scatter_dimension=0, tiled=True)  46.9 us
    all_to_all x1, blocking collectives, shards(): lax.all_to_all(lax.all_to_all(token_slots, 'ep', split_axis=0, concat_axi...  35.5 us
    all_to_all x1, blocking collectives, shards(): lax.all_to_all(cotangent_slots, 'ep', split_axis=0, concat_axis=0, tiled=...  31.9 us
    all_to_all x1, waiting for transfers between devices, shards(): lax.all_to_all(token_slots, 'ep', split_axis=0, concat_axis=0, tiled=True)  25.7 us
    all_gather x1, blocking collectives, shards(): shard_piece = lax.all_gather(update, 'rep', axis=0, tiled=True)  24.8 us
    all_to_all x1, waiting for transfers between devices, shards(): lax.all_to_all(lax.all_to_all(cotangent_slots, 'ep', split_axis=0, concat...  23.4 us
    all_to_all x1, starting transfers between devices, shards(): lax.all_to_all(token_slots, 'ep', split_axis=0, concat_axis=0, tiled=True)  16.8 us
  transfers between devices with their start and end apart: 4, of which 4 were waited for; matrix products, arithmetic and copies ran while one was open for 1% of the time, Pallas kernels for 0%

commit v1 on v0

v1 whole, which is shorter than its diff:
```python
import functools

import jax
import jax.numpy as jnp
from jax import lax
from jax.experimental import pallas as pl
from jax.experimental.pallas import tpu as pltpu
from jax.sharding import PartitionSpec as P

beta_one = 0.9
beta_two = 0.999
adam_step = 1000.0
adam_eps = 1e-08

MESH = pl.DeviceIdType.MESH
BF16 = jnp.bfloat16
F32 = jnp.float32

BLOCKS = 8
SUB = 16
CHUNK = 8
RANK = 512
FEAT = 256
MODEL = 2048
FF = 768
OWN = 64

SLOTS = (
    (0, 0), (0, 1), (1, 0), (1, 1), (-1, 0), (-1, 1), (2, 0), (2, 1),
    (-2, 0), (-2, 1), (3, 0), (3, 1), (-3, 0), (-3, 1), (4, 0), (4, 1),
)
TOKEN_ORDER = (2, 4, 3, 5, 6, 7, 1, 14, 15, 10, 12, 11, 13, 8, 9)
COT_FIRST = (10, 12, 11, 13, 2, 4, 3, 5, 1)
COT_LATER = (6, 7, 14, 15, 8, 9)


def kernel(
    dest_ref, tok_hbm, cot_hbm, gate_hbm, up_hbm, basis_hbm, m1_hbm, m2_hbm,
    m1_out, m2_out, delta_out,
    gate_v, up_v, basis_v, basis_t, cot_v, m1_v, m2_v, xtok,
    csend, crecv, tsend, trecv, hidden, pt, grad, gsend, grecv, upd,
    local_sem, xs, xr, cs, cr, ts, tr, ps, pr, gs, gr, us, ur,
):
    e = lax.axis_index("ep")
    r = lax.axis_index("rep")
    o = lax.axis_index("opt")
    z, c = lax.div(e, 2), lax.rem(e, 2)

    def ep_of(q):
        dz, dc = SLOTS[q]
        core = 1 - c if dc else c
        return lax.rem(z + (dz + 8), 8) * 2 + core

    def turn(axis_index, k):
        return lax.rem(axis_index + k, 8)

    own_features = pl.ds(pl.multiple_of(o * FEAT, FEAT), FEAT)
    loads = [
        pltpu.make_async_copy(cot_hbm, cot_v, local_sem.at[0]),
        pltpu.make_async_copy(tok_hbm.at[:, o], xtok.at[:, :, own_features], local_sem.at[1]),
        pltpu.make_async_copy(basis_hbm.at[0], basis_v, local_sem.at[2]),
        pltpu.make_async_copy(gate_hbm.at[0], gate_v, local_sem.at[3]),
        pltpu.make_async_copy(up_hbm.at[0], up_v, local_sem.at[4]),
        pltpu.make_async_copy(m1_hbm.at[0], m1_v, local_sem.at[5]),
        pltpu.make_async_copy(m2_hbm.at[0], m2_v, local_sem.at[6]),
    ]
    for load in loads:
        load.start()

    barrier = pltpu.get_barrier_semaphore()
    for k in range(1, 8):
        pl.semaphore_signal(barrier, inc=1, device_id={"opt": turn(o, k)}, device_id_type=MESH)
        pl.semaphore_signal(barrier, inc=1, device_id={"rep": turn(r, k)}, device_id_type=MESH)
    for q in range(1, 16):
        pl.semaphore_signal(barrier, inc=1, device_id={"ep": ep_of(q)}, device_id_type=MESH)
    pl.semaphore_wait(barrier, 29)

    def x_copy(k):
        return pltpu.make_async_remote_copy(
            src_ref=tok_hbm.at[:, turn(o, k)],
            dst_ref=xtok.at[:, :, own_features],
            send_sem=xs.at[k],
            recv_sem=xr.at[k],
            device_id={"opt": turn(o, k)},
            device_id_type=MESH,
        )

    x_copies = [x_copy(k) for k in range(1, 8)]
    for copy in x_copies:
        copy.start()

    dest = [dest_ref[r, b, e] for b in range(BLOCKS)]

    def block_for(q):
        target = ep_of(q)
        index, found = jnp.int32(0), jnp.int32(0)
        for b in range(BLOCKS):
            hit = dest[b] == target
            index = jnp.where(hit, b, index)
            found = jnp.where(hit, 1, found)
        return index, found

    def cot_copy(q):
        return pltpu.make_async_remote_copy(
            src_ref=csend.at[q],
            dst_ref=crecv.at[q // CHUNK, :, q % CHUNK],
            send_sem=cs.at[q],
            recv_sem=cr.at[q],
            device_id={"ep": ep_of(q)},
            device_id_type=MESH,
        )

    def token_copy(q):
        return pltpu.make_async_remote_copy(
            src_ref=tsend.at[q],
            dst_ref=trecv.at[q // CHUNK, q % CHUNK],
            send_sem=ts.at[q],
            recv_sem=tr.at[q],
            device_id={"ep": ep_of(q)},
            device_id_type=MESH,
        )

    def send_cot(q):
        index, _ = block_for(q)
        csend[q] = cot_v[index]
        cot_copy(q).start()

    def token_slot(q):
        index, found = block_for(q)
        rows = xtok[index]
        return jnp.where(found > 0, rows, jnp.zeros_like(rows))

    loads[0].wait()
    for q in COT_FIRST:
        send_cot(q)
    crecv[0, :, 0] = cot_v[block_for(0)[0]]

    loads[2].wait()
    for part in range(3):
        rows = pl.ds(part * 256, 256)
        basis_t[:, rows] = basis_v[rows, :].T

    loads[1].wait()
    for copy in x_copies:
        copy.wait_recv()
    for q in TOKEN_ORDER:
        tsend[q] = token_slot(q)
        token_copy(q).start()
    trecv[0, 0] = token_slot(0)

    loads[3].wait()
    loads[4].wait()

    own_columns = pl.ds(pl.multiple_of(o * 128, 128), 128)

    def pt_copy(chunk, k):
        return pltpu.make_async_remote_copy(
            src_ref=pt.at[chunk, :, own_columns],
            dst_ref=pt.at[chunk, :, own_columns],
            send_sem=ps.at[chunk, k],
            recv_sem=pr.at[chunk, k],
            device_id={"opt": turn(o, k)},
            device_id_type=MESH,
        )

    def project(chunk):
        rows = trecv[chunk].reshape(CHUNK * SUB, MODEL)
        for part in range(3):
            columns = pl.ds(part * 256, 256)
            gate = jnp.dot(rows, gate_v[:, columns], preferred_element_type=F32)
            up = jnp.dot(rows, up_v[:, columns], preferred_element_type=F32)
            hidden[:, columns] = (gate / (1.0 + jnp.exp(-gate)) * up).astype(BF16)
        projected = lax.dot_general(
            basis_t[...], hidden[...], (((1,), (1,)), ((), ())), preferred_element_type=F32
        )
        pt[chunk, :, own_columns] = projected.astype(BF16)
        for k in range(1, 8):
            pt_copy(chunk, k).start()

    for q in range(1, CHUNK):
        token_copy(q).wait_recv()
    project(0)
    for q in COT_LATER:
        send_cot(q)
    for q in range(CHUNK, 2 * CHUNK):
        token_copy(q).wait_recv()
    project(1)

    def contract(chunk):
        return jnp.dot(
            pt[chunk],
            crecv[chunk].reshape(8 * CHUNK * SUB, FEAT),
            preferred_element_type=F32,
        )

    for q in range(1, CHUNK):
        cot_copy(q).wait_recv()
    for k in range(1, 8):
        pt_copy(0, k).wait_recv()
    grad[...] = contract(0)
    for q in range(CHUNK, 2 * CHUNK):
        cot_copy(q).wait_recv()
    for k in range(1, 8):
        pt_copy(1, k).wait_recv()
    grad[...] += contract(1)
    gsend[...] = grad[...].astype(BF16)

    def grad_copy(k):
        rows = pl.ds(pl.multiple_of(turn(r, k) * OWN, OWN), OWN)
        return pltpu.make_async_remote_copy(
            src_ref=gsend.at[rows],
            dst_ref=grecv.at[k],
            send_sem=gs.at[k],
            recv_sem=gr.at[k],
            device_id={"rep": turn(r, k)},
            device_id_type=MESH,
        )

    for k in (4, 3, 5, 2, 6, 1, 7):
        grad_copy(k).start()
    own_rows = pl.ds(pl.multiple_of(r * OWN, OWN), OWN)
    gradient = grad[own_rows, :]
    loads[5].wait()
    loads[6].wait()
    for k in range(1, 8):
        grad_copy(k).wait_recv()
    for k in range(1, 8):
        gradient += grecv[k].astype(F32)

    first_moment = beta_one * m1_v[...] + (1.0 - beta_one) * gradient
    second_moment = beta_two * m2_v[...] + (1.0 - beta_two) * gradient * gradient
    m1_out[0] = first_moment
    m2_out[0] = second_moment
    scaled_first = first_moment / (1.0 - beta_one**adam_step)
    scaled_second = second_moment / (1.0 - beta_two**adam_step)
    upd[own_rows, :] = (-scaled_first / (jnp.sqrt(scaled_second) + adam_eps)).astype(BF16)

    def update_copy(k):
        return pltpu.make_async_remote_copy(
            src_ref=upd.at[own_rows],
            dst_ref=upd.at[own_rows],
            send_sem=us.at[k],
            recv_sem=ur.at[k],
            device_id={"rep": turn(r, k)},
            device_id_type=MESH,
        )

    for k in (4, 3, 5, 2, 6, 1, 7):
        update_copy(k).start()
    for copy in x_copies:
        copy.wait_send()
    for q in range(1, 16):
        cot_copy(q).wait_send()
        token_copy(q).wait_send()
    for k in range(1, 8):
        pt_copy(0, k).wait_send()
        pt_copy(1, k).wait_send()
        grad_copy(k).wait_send()
    for k in range(1, 8):
        update_copy(k).wait_recv()
    delta_out[0] = jnp.dot(basis_v[...], upd[...], preferred_element_type=F32).astype(BF16)
    for k in range(1, 8):
        update_copy(k).wait_send()


def shards(
    incoming_tokens,
    cotangent,
    block_dest,
    gate_weight,
    up_weight,
    basis,
    moment_first,
    moment_second,
):
    tokens = incoming_tokens.reshape(BLOCKS, 8, SUB, FEAT)
    cot = cotangent.reshape(BLOCKS, 8, SUB, FEAT)
    hbm = pl.BlockSpec(memory_space=pl.ANY)
    vmem = pl.BlockSpec(memory_space=pltpu.VMEM)
    dma = pltpu.SemaphoreType.DMA
    return pl.pallas_call(
        kernel,
        out_shape=(
            jax.ShapeDtypeStruct((1, OWN, FEAT), F32),
            jax.ShapeDtypeStruct((1, OWN, FEAT), F32),
            jax.ShapeDtypeStruct((1, FF, FEAT), BF16),
        ),
        in_specs=[pl.BlockSpec(memory_space=pltpu.SMEM)] + [hbm] * 7,
        out_specs=(vmem, vmem, vmem),
        scratch_shapes=[
            pltpu.VMEM((MODEL, FF), BF16),
            pltpu.VMEM((MODEL, FF), BF16),
            pltpu.VMEM((FF, RANK), BF16),
            pltpu.VMEM((RANK, FF), BF16),
            pltpu.VMEM((BLOCKS, 8, SUB, FEAT), BF16),
            pltpu.VMEM((OWN, FEAT), F32),
            pltpu.VMEM((OWN, FEAT), F32),
            pltpu.VMEM((BLOCKS, SUB, MODEL), BF16),
            pltpu.VMEM((16, 8, SUB, FEAT), BF16),
            pltpu.VMEM((2, 8, CHUNK, SUB, FEAT), BF16),
            pltpu.VMEM((16, SUB, MODEL), BF16),
            pltpu.VMEM((2, CHUNK, SUB, MODEL), BF16),
            pltpu.VMEM((CHUNK * SUB, FF), BF16),
            pltpu.VMEM((2, RANK, 8 * CHUNK * SUB), BF16),
            pltpu.VMEM((RANK, FEAT), F32),
            pltpu.VMEM((RANK, FEAT), BF16),
            pltpu.VMEM((8, OWN, FEAT), BF16),
            pltpu.VMEM((RANK, FEAT), BF16),
            dma((7,)),
            dma((8,)), dma((8,)),
            dma((16,)), dma((16,)),
            dma((16,)), dma((16,)),
            dma((2, 8)), dma((2, 8)),
            dma((8,)), dma((8,)),
            dma((8,)), dma((8,)),
        ],
        compiler_params=pltpu.CompilerParams(
            collective_id=0, has_side_effects=True, vmem_limit_bytes=63 * 1024 * 1024
        ),
    )(jnp.transpose(block_dest, (1, 2, 0)), tokens, cot, gate_weight, up_weight, basis, moment_first, moment_second)


def solution(mesh):
    in_specs = (
        P("ep", "rep", None, None, "opt"),
        P("ep", "rep", None, None, "opt"),
        P(),
        P("ep", None, None),
        P("ep", None, None),
        P("ep", None, None),
        P("ep", "rep", "opt"),
        P("ep", "rep", "opt"),
    )
    out_specs = (P("ep", "rep", "opt"), P("ep", "rep", "opt"), P("ep", None, "opt"))
    return jax.shard_map(shards, mesh=mesh, in_specs=in_specs, out_specs=out_specs, check_vma=False)
```

time: 305 us -> 126 us (0.41)
  the two profiles are of different devices: /device:TPU:2 before, /device:TPU:132 now
where the time goes in v1:
time: 126 us
  Pallas kernels  120 us (95%)
  local copies, waits for them, and re-layouts  4.71 us (4%)
    pallas_call x1, Pallas kernels, shards(): pl.pallas_call(kernel, out_shape=(jax.ShapeDtypeStruct((1, OWN, FEAT), F3...  120 us
    unnamed x3, local copies, waits for them, and re-layouts  4.71 us

profile of v1, /device:TPU:132, one launch (start us, length us, event | category | flops | bytes accessed | tf_op | source)
XLA Modules:
  0.0 125.6 jit_solution(16945705300768774057)
XLA Ops:
  0.6 120.3 %shard_map.103 = (f32[1,64,256]{2,1,0:T(8,128)}, f32[1,64,256]{2,1,0:T(8,128)}, bf16[1,768,256]{2,1,0:T(8,128)(2,1)}) custom-call(s32[8,8,16]{2,1,0:T(8,128)} %bitcast.5, bf16[8,8,16,256]{3,2,1,0:T(8,128)(2,1)} %bitcast.3, bf16[8,8,16,256]{3,2,1,0:T(8,128)(2,1)} %bitcast.4, bf16[1,2048,768]{2,1,0:T(8,128)(2,1)} %gate_hbm.1, bf16[1,2048,768]{2,1,0:T(8,128)(2,1)} %up_hbm.1, ...), custom_call_target="tpu_custom_call" | custom-call | tf_op jit(solution)/shard_map/pallas_call | solution.py:281
  120.9 1.5 %copy.14 = f32[1,64,256]{2,1,0:T(8,128)} copy(f32[1,64,256]{2,1,0:T(8,128)} %get-tuple-element.6) | data formatting | bytes 131072
  122.4 1.5 %copy.15 = f32[1,64,256]{2,1,0:T(8,128)} copy(f32[1,64,256]{2,1,0:T(8,128)} %get-tuple-element.7) | data formatting | bytes 131072
  123.9 1.8 %copy.16 = bf16[1,768,256]{2,1,0:T(8,128)(2,1)} copy(bf16[1,768,256]{2,1,0:T(8,128)(2,1)} %get-tuple-element.8) | data formatting | bytes 786432

commit v2 on v1

--- a/solution.py
+++ b/solution.py
@@ -18,7 +18,6 @@
 
 BLOCKS = 8
 SUB = 16
-CHUNK = 8
 RANK = 512
 FEAT = 256
 MODEL = 2048
@@ -26,19 +25,40 @@
 OWN = 64
 
 SLOTS = (
-    (0, 0), (0, 1), (1, 0), (1, 1), (-1, 0), (-1, 1), (2, 0), (2, 1),
-    (-2, 0), (-2, 1), (3, 0), (3, 1), (-3, 0), (-3, 1), (4, 0), (4, 1),
+    (0, 0), (0, 1), (1, 0), (1, 1), (-1, 0), (-1, 1),
+    (2, 0), (2, 1), (-2, 0), (-2, 1),
+    (3, 0), (3, 1), (-3, 0), (-3, 1),
+    (4, 0), (4, 1),
 )
-TOKEN_ORDER = (2, 4, 3, 5, 6, 7, 1, 14, 15, 10, 12, 11, 13, 8, 9)
+CHUNKS = ((0, 6), (6, 10), (10, 14), (14, 16))
+LAST = len(CHUNKS) - 1
+PLACE = {q: (n, q - low) for n, (low, high) in enumerate(CHUNKS) for q in range(low, high)}
+TOKEN_ORDER = (2, 4, 3, 5, 1, 6, 8, 7, 9, 10, 12, 11, 13, 14, 15)
 COT_FIRST = (10, 12, 11, 13, 2, 4, 3, 5, 1)
-COT_LATER = (6, 7, 14, 15, 8, 9)
+COT_LATER = (6, 8, 7, 9, 14, 15)
+DIRECT = (1, 7, 2, 6)
+DIRECT_ALL = (4, 3, 5, 2, 6, 1, 7)
+
+
+def adam(moment_first, moment_second, gradient):
+    first_moment = beta_one * moment_first + (1.0 - beta_one) * gradient
+    second_moment = beta_two * moment_second + (1.0 - beta_two) * gradient * gradient
+    scaled_first = first_moment / (1.0 - beta_one**adam_step)
+    scaled_second = second_moment / (1.0 - beta_two**adam_step)
+    update = (-scaled_first / (jnp.sqrt(scaled_second) + adam_eps)).astype(BF16)
+    return first_moment, second_moment, update
+
+
+def rows_of(chunk):
+    low, high = CHUNKS[chunk]
+    return (high - low) * SUB
 
 
 def kernel(
     dest_ref, tok_hbm, cot_hbm, gate_hbm, up_hbm, basis_hbm, m1_hbm, m2_hbm,
-    m1_out, m2_out, delta_out,
-    gate_v, up_v, basis_v, basis_t, cot_v, m1_v, m2_v, xtok,
-    csend, crecv, tsend, trecv, hidden, pt, grad, gsend, grecv, upd,
+    gradient_out, update_out,
+    gate_v, up_v, basis_v, cot_v, m1_v, m2_v, xtok, csend, tsend, hidden, grad, gsend, grecv, upd,
+    crecv, trecv, proj,
     local_sem, xs, xr, cs, cr, ts, tr, ps, pr, gs, gr, us, ur,
 ):
     e = lax.axis_index("ep")
@@ -103,7 +123,7 @@
     def cot_copy(q):
         return pltpu.make_async_remote_copy(
             src_ref=csend.at[q],
-            dst_ref=crecv.at[q // CHUNK, :, q % CHUNK],
+            dst_ref=crecv[PLACE[q][0]].at[:, PLACE[q][1]],
             send_sem=cs.at[q],
             recv_sem=cr.at[q],
             device_id={"ep": ep_of(q)},
@@ -113,7 +133,7 @@
     def token_copy(q):
         return pltpu.make_async_remote_copy(
             src_ref=tsend.at[q],
-            dst_ref=trecv.at[q // CHUNK, q % CHUNK],
+            dst_ref=trecv[PLACE[q][0]].at[PLACE[q][1]],
             send_sem=ts.at[q],
             recv_sem=tr.at[q],
             device_id={"ep": ep_of(q)},
@@ -133,12 +153,7 @@
     loads[0].wait()
     for q in COT_FIRST:
         send_cot(q)
-    crecv[0, :, 0] = cot_v[block_for(0)[0]]
-
-    loads[2].wait()
-    for part in range(3):
-        rows = pl.ds(part * 256, 256)
-        basis_t[:, rows] = basis_v[rows, :].T
+    crecv[0][:, 0] = cot_v[block_for(0)[0]]
 
     loads[1].wait()
     for copy in x_copies:
@@ -146,63 +161,103 @@
     for q in TOKEN_ORDER:
         tsend[q] = token_slot(q)
         token_copy(q).start()
-    trecv[0, 0] = token_slot(0)
+    trecv[0][0] = token_slot(0)
 
     loads[3].wait()
     loads[4].wait()
 
-    own_columns = pl.ds(pl.multiple_of(o * 128, 128), 128)
-
-    def pt_copy(chunk, k):
-        return pltpu.make_async_remote_copy(
-            src_ref=pt.at[chunk, :, own_columns],
-            dst_ref=pt.at[chunk, :, own_columns],
+    loads[2].wait()
+
+    def direct(chunk, k):
+        return pltpu.make_async_remote_copy(
+            src_ref=proj[chunk].at[o],
+            dst_ref=proj[chunk].at[o],
             send_sem=ps.at[chunk, k],
             recv_sem=pr.at[chunk, k],
             device_id={"opt": turn(o, k)},
             device_id_type=MESH,
         )
 
+    def forwards(chunk):
+        half = rows_of(chunk) // 2
+        moves = (
+            (turn(o, 6), 0, 2 * half, 1, 3),
+            (turn(o, 2), 0, 2 * half, 7, 5),
+            (turn(o, 6), 0, half, 2, 4),
+            (turn(o, 2), half, half, 6, 0),
+        )
+        return [
+            pltpu.make_async_remote_copy(
+                src_ref=proj[chunk].at[source, pl.ds(low, size)],
+                dst_ref=proj[chunk].at[source, pl.ds(low, size)],
+                send_sem=ps.at[chunk, sem],
+                recv_sem=pr.at[chunk, sem],
+                device_id={"opt": turn(o, k)},
+                device_id_type=MESH,
+            )
+            for source, low, size, k, sem in moves
+        ]
+
     def project(chunk):
-        rows = trecv[chunk].reshape(CHUNK * SUB, MODEL)
+        for q in range(*CHUNKS[chunk]):
+            if q:
+                token_copy(q).wait_recv()
+        rows = trecv[chunk][...].reshape(rows_of(chunk), MODEL)
+        local = pl.ds(0, rows_of(chunk))
         for part in range(3):
             columns = pl.ds(part * 256, 256)
             gate = jnp.dot(rows, gate_v[:, columns], preferred_element_type=F32)
             up = jnp.dot(rows, up_v[:, columns], preferred_element_type=F32)
-            hidden[:, columns] = (gate / (1.0 + jnp.exp(-gate)) * up).astype(BF16)
-        projected = lax.dot_general(
-            basis_t[...], hidden[...], (((1,), (1,)), ((), ())), preferred_element_type=F32
-        )
-        pt[chunk, :, own_columns] = projected.astype(BF16)
-        for k in range(1, 8):
-            pt_copy(chunk, k).start()
-
-    for q in range(1, CHUNK):
-        token_copy(q).wait_recv()
+            hidden[local, columns] = (gate / (1.0 + jnp.exp(-gate)) * up).astype(BF16)
+        projected = jnp.dot(hidden[local, :], basis_v[...], preferred_element_type=F32)
+        proj[chunk][o] = projected.astype(BF16)
+
+    def send_direct(chunk):
+        for k in DIRECT_ALL if chunk == LAST else DIRECT:
+            direct(chunk, k).start()
+
+    def pass_on(chunk):
+        direct(chunk, 2).wait_recv()
+        direct(chunk, 6).wait_recv()
+        for copy in forwards(chunk):
+            copy.start()
+
+    def contract(chunk):
+        for q in range(*CHUNKS[chunk]):
+            if q:
+                cot_copy(q).wait_recv()
+        if chunk == LAST:
+            for k in DIRECT_ALL:
+                direct(chunk, k).wait_recv()
+        else:
+            direct(chunk, 1).wait_recv()
+            direct(chunk, 7).wait_recv()
+            for copy in forwards(chunk):
+                copy.wait_recv()
+        return lax.dot_general(
+            proj[chunk][...].reshape(8 * rows_of(chunk), RANK),
+            crecv[chunk][...].reshape(8 * rows_of(chunk), FEAT),
+            (((0,), (0,)), ((), ())),
+            preferred_element_type=F32,
+        )
+
     project(0)
+    send_direct(0)
+    project(1)
+    pass_on(0)
+    send_direct(1)
     for q in COT_LATER:
         send_cot(q)
-    for q in range(CHUNK, 2 * CHUNK):
-        token_copy(q).wait_recv()
-    project(1)
-
-    def contract(chunk):
-        return jnp.dot(
-            pt[chunk],
-            crecv[chunk].reshape(8 * CHUNK * SUB, FEAT),
-            preferred_element_type=F32,
-        )
-
-    for q in range(1, CHUNK):
-        cot_copy(q).wait_recv()
-    for k in range(1, 8):
-        pt_copy(0, k).wait_recv()
+    project(2)
+    pass_on(1)
+    send_direct(2)
+    project(3)
+    send_direct(3)
+    pass_on(2)
     grad[...] = contract(0)
-    for q in range(CHUNK, 2 * CHUNK):
-        cot_copy(q).wait_recv()
-    for k in range(1, 8):
-        pt_copy(1, k).wait_recv()
     grad[...] += contract(1)
+    grad[...] += contract(2)
+    grad[...] += contract(3)
     gsend[...] = grad[...].astype(BF16)
 
     def grad_copy(k):
@@ -227,13 +282,8 @@
     for k in range(1, 8):
         gradient += grecv[k].astype(F32)
 
-    first_moment = beta_one * m1_v[...] + (1.0 - beta_one) * gradient
-    second_moment = beta_two * m2_v[...] + (1.0 - beta_two) * gradient * gradient
-    m1_out[0] = first_moment
-    m2_out[0] = second_moment
-    scaled_first = first_moment / (1.0 - beta_one**adam_step)
-    scaled_second = second_moment / (1.0 - beta_two**adam_step)
-    upd[own_rows, :] = (-scaled_first / (jnp.sqrt(scaled_second) + adam_eps)).astype(BF16)
+    gradient_out[...] = gradient
+    upd[own_rows, :] = adam(m1_v[...], m2_v[...], gradient)[2]
 
     def update_copy(k):
         return pltpu.make_async_remote_copy(
@@ -252,15 +302,26 @@
     for q in range(1, 16):
         cot_copy(q).wait_send()
         token_copy(q).wait_send()
-    for k in range(1, 8):
-        pt_copy(0, k).wait_send()
-        pt_copy(1, k).wait_send()
+    for chunk in range(LAST):
+        for k in DIRECT:
+            direct(chunk, k).wait_send()
+        for copy in forwards(chunk):
+            copy.wait_send()
+    for k in range(1, 8):
+        direct(LAST, k).wait_send()
         grad_copy(k).wait_send()
     for k in range(1, 8):
         update_copy(k).wait_recv()
-    delta_out[0] = jnp.dot(basis_v[...], upd[...], preferred_element_type=F32).astype(BF16)
+    update_out[...] = upd[...]
     for k in range(1, 8):
         update_copy(k).wait_send()
+
+
+def finish(gradient_ref, update_ref, basis_ref, m1_ref, m2_ref, m1_out, m2_out, delta_out):
+    first_moment, second_moment, _ = adam(m1_ref[0], m2_ref[0], gradient_ref[...])
+    m1_out[0] = first_moment
+    m2_out[0] = second_moment
+    delta_out[0] = jnp.dot(basis_ref[0], update_ref[...], preferred_element_type=F32).astype(BF16)
 
 
 def shards(
@@ -278,46 +339,64 @@
     hbm = pl.BlockSpec(memory_space=pl.ANY)
     vmem = pl.BlockSpec(memory_space=pltpu.VMEM)
     dma = pltpu.SemaphoreType.DMA
-    return pl.pallas_call(
+    gradient, update = pl.pallas_call(
         kernel,
         out_shape=(
-            jax.ShapeDtypeStruct((1, OWN, FEAT), F32),
-            jax.ShapeDtypeStruct((1, OWN, FEAT), F32),
-            jax.ShapeDtypeStruct((1, FF, FEAT), BF16),
+            jax.ShapeDtypeStruct((OWN, FEAT), F32),
+            jax.ShapeDtypeStruct((RANK, FEAT), BF16),
         ),
         in_specs=[pl.BlockSpec(memory_space=pltpu.SMEM)] + [hbm] * 7,
-        out_specs=(vmem, vmem, vmem),
+        out_specs=(vmem, vmem),
         scratch_shapes=[
             pltpu.VMEM((MODEL, FF), BF16),
             pltpu.VMEM((MODEL, FF), BF16),
             pltpu.VMEM((FF, RANK), BF16),
-            pltpu.VMEM((RANK, FF), BF16),
             pltpu.VMEM((BLOCKS, 8, SUB, FEAT), BF16),
             pltpu.VMEM((OWN, FEAT), F32),
             pltpu.VMEM((OWN, FEAT), F32),
             pltpu.VMEM((BLOCKS, SUB, MODEL), BF16),
             pltpu.VMEM((16, 8, SUB, FEAT), BF16),
-            pltpu.VMEM((2, 8, CHUNK, SUB, FEAT), BF16),
             pltpu.VMEM((16, SUB, MODEL), BF16),
-            pltpu.VMEM((2, CHUNK, SUB, MODEL), BF16),
-            pltpu.VMEM((CHUNK * SUB, FF), BF16),
-            pltpu.VMEM((2, RANK, 8 * CHUNK * SUB), BF16),
+            pltpu.VMEM((rows_of(0), FF), BF16),
             pltpu.VMEM((RANK, FEAT), F32),
             pltpu.VMEM((RANK, FEAT), BF16),
             pltpu.VMEM((8, OWN, FEAT), BF16),
             pltpu.VMEM((RANK, FEAT), BF16),
+            [pltpu.VMEM((8, high - low, SUB, FEAT), BF16) for low, high in CHUNKS],
+            [pltpu.VMEM((high - low, SUB, MODEL), BF16) for low, high in CHUNKS],
+            [pltpu.VMEM((8, (high - low) * SUB, RANK), BF16) for low, high in CHUNKS],
             dma((7,)),
             dma((8,)), dma((8,)),
             dma((16,)), dma((16,)),
             dma((16,)), dma((16,)),
-            dma((2, 8)), dma((2, 8)),
+            dma((len(CHUNKS), 8)), dma((len(CHUNKS), 8)),
             dma((8,)), dma((8,)),
             dma((8,)), dma((8,)),
         ],
         compiler_params=pltpu.CompilerParams(
             collective_id=0, has_side_effects=True, vmem_limit_bytes=63 * 1024 * 1024
         ),
-    )(jnp.transpose(block_dest, (1, 2, 0)), tokens, cot, gate_weight, up_weight, basis, moment_first, moment_second)
+    )(
+        jnp.transpose(block_dest, (1, 2, 0)),
+        tokens,
+        cot,
+        gate_weight,
+        up_weight,
+        basis,
+        moment_first,
+        moment_second,
+    )
+    return pl.pallas_call(
+        finish,
+        out_shape=(
+            jax.ShapeDtypeStruct((1, OWN, FEAT), F32),
+            jax.ShapeDtypeStruct((1, OWN, FEAT), F32),
+            jax.ShapeDtypeStruct((1, FF, FEAT), BF16),
+        ),
+        in_specs=[vmem] * 5,
+        out_specs=(vmem, vmem, vmem),
+        cost_estimate=pl.CostEstimate(flops=2 * FF * RANK * FEAT, bytes_accessed=2**21, transcendentals=0),
+    )(gradient, update, basis, moment_first, moment_second)
 
 
 def solution(mesh):

time: 126 us -> 104 us (0.83)
  the two profiles are of different devices: /device:TPU:132 before, /device:TPU:5 now
where the time goes in v2:
time: 104 us
  Pallas kernels  103 us (99%)
    pallas_call x1, Pallas kernels, shards(): pl.pallas_call(kernel, out_shape=(jax.ShapeDtypeStruct((OWN, FEAT), F32),...  101 us
    pallas_call x1, Pallas kernels, shards(): pl.pallas_call(finish, out_shape=(jax.ShapeDtypeStruct((1, OWN, FEAT), F3...  2.41 us

profile of v2, /device:TPU:5, one launch (start us, length us, event | category | flops | bytes accessed | tf_op | source)
XLA Modules:
  0.0 104.1 jit_solution(17286659733044159786)
XLA Ops:
  0.6 101.1 %shard_map.103 = (f32[64,256]{1,0:T(8,128)}, bf16[512,256]{1,0:T(8,128)(2,1)}) custom-call(s32[8,8,16]{2,1,0:T(8,128)} %bitcast.5, bf16[8,8,16,256]{3,2,1,0:T(8,128)(2,1)} %bitcast.3, bf16[8,8,16,256]{3,2,1,0:T(8,128)(2,1)} %bitcast.4, bf16[1,2048,768]{2,1,0:T(8,128)(2,1)} %gate_hbm.1, bf16[1,2048,768]{2,1,0:T(8,128)(2,1)} %up_hbm.1, ...), custom_call_target="tpu_custom_call" | custom-call | tf_op jit(solution)/shard_map/pallas_call | solution.py:342
  101.7 2.4 %shard_map.104 = (f32[1,64,256]{2,1,0:T(8,128)}, f32[1,64,256]{2,1,0:T(8,128)}, bf16[1,768,256]{2,1,0:T(8,128)(2,1)}) custom-call(f32[64,256]{1,0:T(8,128)} %get-tuple-element.5.gradient_ref, bf16[512,256]{1,0:T(8,128)(2,1)} %get-tuple-element.6.update_ref, bf16[1,768,512]{2,1,0:T(8,128)(2,1)} %basis_ref.1, f32[1,64,256]{2,1,0:T(8,128)} %m1_ref.1, ...), custom_call_target="tpu_custom_call" | custom-call | flops 201326592 | bytes 2097152 | tf_op jit(solution)/shard_map/pallas_call | solution.py:389

commit v3 on v2

--- a/solution.py
+++ b/solution.py
@@ -31,13 +31,43 @@
     (4, 0), (4, 1),
 )
 CHUNKS = ((0, 6), (6, 10), (10, 14), (14, 16))
-LAST = len(CHUNKS) - 1
 PLACE = {q: (n, q - low) for n, (low, high) in enumerate(CHUNKS) for q in range(low, high)}
-TOKEN_ORDER = (2, 4, 3, 5, 1, 6, 8, 7, 9, 10, 12, 11, 13, 14, 15)
-COT_FIRST = (10, 12, 11, 13, 2, 4, 3, 5, 1)
-COT_LATER = (6, 8, 7, 9, 14, 15)
+TOKEN_ORDER = ((2, 4, 3, 5, 1), (6, 8, 7, 9), (10, 12, 11, 13), (14, 15))
+COT_FIRST = (10, 12, 11, 13, 6, 8, 7, 9, 2, 4, 3, 5, 1)
+COT_LATER = (14, 15)
 DIRECT = (1, 7, 2, 6)
-DIRECT_ALL = (4, 3, 5, 2, 6, 1, 7)
+REP_HOPS = (4, 3, 5, 2, 6, 1, 7)
+SCHEDULE = (
+    ("tokens", 0), ("tokens", 1),
+    ("project", 0), ("hop", 0, 0), ("tokens", 2),
+    ("project", 1), ("hop", 1, 0), ("hop", 0, 1), ("tokens", 3), ("hop", 0, 2), ("hop", 1, 1),
+    ("project", 2), ("direct", 2), ("hop", 0, 3), ("hop", 1, 2),
+    ("project", 3), ("direct", 3), ("cot",), ("hop", 1, 3), ("pass", 2), ("pass", 3),
+    ("grad", 0), ("grad", 1), ("grad", 2), ("grad", 3),
+)
+
+
+class Transfers:
+    def __init__(self):
+        self.sends, self.arrivals = {}, {}
+
+    def start(self, name, copy):
+        copy.start()
+        self.sends[name] = self.arrivals[name] = copy
+
+    def sent(self, name):
+        if name in self.sends:
+            self.sends.pop(name).wait_send()
+
+    def arrived(self, name):
+        if name in self.arrivals:
+            self.arrivals.pop(name).wait_recv()
+
+    def finish(self):
+        for name in list(self.arrivals):
+            self.arrived(name)
+        for name in list(self.sends):
+            self.sent(name)
 
 
 def adam(moment_first, moment_second, gradient):
@@ -90,10 +120,11 @@
     barrier = pltpu.get_barrier_semaphore()
     for k in range(1, 8):
         pl.semaphore_signal(barrier, inc=1, device_id={"opt": turn(o, k)}, device_id_type=MESH)
+    for k in REP_HOPS:
         pl.semaphore_signal(barrier, inc=1, device_id={"rep": turn(r, k)}, device_id_type=MESH)
     for q in range(1, 16):
         pl.semaphore_signal(barrier, inc=1, device_id={"ep": ep_of(q)}, device_id_type=MESH)
-    pl.semaphore_wait(barrier, 29)
+    pl.semaphore_wait(barrier, 22 + len(REP_HOPS))
 
     def x_copy(k):
         return pltpu.make_async_remote_copy(
@@ -105,9 +136,9 @@
             device_id_type=MESH,
         )
 
-    x_copies = [x_copy(k) for k in range(1, 8)]
-    for copy in x_copies:
-        copy.start()
+    moving = Transfers()
+    for k in range(1, 8):
+        moving.start(("x", k), x_copy(k))
 
     dest = [dest_ref[r, b, e] for b in range(BLOCKS)]
 
@@ -143,7 +174,7 @@
     def send_cot(q):
         index, _ = block_for(q)
         csend[q] = cot_v[index]
-        cot_copy(q).start()
+        moving.start(("cot", q), cot_copy(q))
 
     def token_slot(q):
         index, found = block_for(q)
@@ -156,17 +187,15 @@
     crecv[0][:, 0] = cot_v[block_for(0)[0]]
 
     loads[1].wait()
-    for copy in x_copies:
-        copy.wait_recv()
-    for q in TOKEN_ORDER:
-        tsend[q] = token_slot(q)
-        token_copy(q).start()
+    for k in range(1, 8):
+        moving.arrived(("x", k))
+
+    def send_tokens(chunk):
+        for q in TOKEN_ORDER[chunk]:
+            tsend[q] = token_slot(q)
+            moving.start(("token", q), token_copy(q))
+
     trecv[0][0] = token_slot(0)
-
-    loads[3].wait()
-    loads[4].wait()
-
-    loads[2].wait()
 
     def direct(chunk, k):
         return pltpu.make_async_remote_copy(
@@ -187,21 +216,30 @@
             (turn(o, 2), half, half, 6, 0),
         )
         return [
-            pltpu.make_async_remote_copy(
-                src_ref=proj[chunk].at[source, pl.ds(low, size)],
-                dst_ref=proj[chunk].at[source, pl.ds(low, size)],
-                send_sem=ps.at[chunk, sem],
-                recv_sem=pr.at[chunk, sem],
-                device_id={"opt": turn(o, k)},
-                device_id_type=MESH,
+            (
+                sem,
+                pltpu.make_async_remote_copy(
+                    src_ref=proj[chunk].at[source, pl.ds(low, size)],
+                    dst_ref=proj[chunk].at[source, pl.ds(low, size)],
+                    send_sem=ps.at[chunk, sem],
+                    recv_sem=pr.at[chunk, sem],
+                    device_id={"opt": turn(o, k)},
+                    device_id_type=MESH,
+                ),
             )
             for source, low, size, k, sem in moves
         ]
 
+    waiting = loads[2:5]
+
+    def weights():
+        while waiting:
+            waiting.pop(0).wait()
+
     def project(chunk):
+        weights()
         for q in range(*CHUNKS[chunk]):
-            if q:
-                token_copy(q).wait_recv()
+            moving.arrived(("token", q))
         rows = trecv[chunk][...].reshape(rows_of(chunk), MODEL)
         local = pl.ds(0, rows_of(chunk))
         for part in range(3):
@@ -213,51 +251,64 @@
         proj[chunk][o] = projected.astype(BF16)
 
     def send_direct(chunk):
-        for k in DIRECT_ALL if chunk == LAST else DIRECT:
-            direct(chunk, k).start()
+        for k in DIRECT:
+            moving.start(("proj", chunk, k), direct(chunk, k))
+
+    def hop(chunk, stage):
+        size = rows_of(chunk)
+        half = size // 2 if stage == 3 else size
+        moving.arrived(("proj", chunk, stage))
+        moving.arrived(("proj", chunk, 8 - stage))
+        for source, low, k, sem in (
+            (turn(o, 8 - stage), 0, 1, stage + 1),
+            (turn(o, stage), size - half, 7, 0 if stage == 3 else 7 - stage),
+        ):
+            piece = proj[chunk].at[source, pl.ds(low, half)]
+            copy = pltpu.make_async_remote_copy(
+                src_ref=piece,
+                dst_ref=piece,
+                send_sem=ps.at[chunk, sem],
+                recv_sem=pr.at[chunk, sem],
+                device_id={"opt": turn(o, k)},
+                device_id_type=MESH,
+            )
+            moving.start(("proj", chunk, sem), copy)
 
     def pass_on(chunk):
-        direct(chunk, 2).wait_recv()
-        direct(chunk, 6).wait_recv()
-        for copy in forwards(chunk):
-            copy.start()
+        moving.arrived(("proj", chunk, 2))
+        moving.arrived(("proj", chunk, 6))
+        for sem, copy in forwards(chunk):
+            moving.start(("proj", chunk, sem), copy)
 
     def contract(chunk):
         for q in range(*CHUNKS[chunk]):
-            if q:
-                cot_copy(q).wait_recv()
-        if chunk == LAST:
-            for k in DIRECT_ALL:
-                direct(chunk, k).wait_recv()
-        else:
-            direct(chunk, 1).wait_recv()
-            direct(chunk, 7).wait_recv()
-            for copy in forwards(chunk):
-                copy.wait_recv()
-        return lax.dot_general(
+            moving.arrived(("cot", q))
+        for k in range(8):
+            moving.arrived(("proj", chunk, k))
+        term = lax.dot_general(
             proj[chunk][...].reshape(8 * rows_of(chunk), RANK),
             crecv[chunk][...].reshape(8 * rows_of(chunk), FEAT),
             (((0,), (0,)), ((), ())),
             preferred_element_type=F32,
         )
-
-    project(0)
-    send_direct(0)
-    project(1)
-    pass_on(0)
-    send_direct(1)
-    for q in COT_LATER:
-        send_cot(q)
-    project(2)
-    pass_on(1)
-    send_direct(2)
-    project(3)
-    send_direct(3)
-    pass_on(2)
-    grad[...] = contract(0)
-    grad[...] += contract(1)
-    grad[...] += contract(2)
-    grad[...] += contract(3)
+        grad[...] = term if chunk == 0 else grad[...] + term
+
+    def send_cots():
+        for q in COT_LATER:
+            send_cot(q)
+
+    run = {
+        "tokens": send_tokens,
+        "project": project,
+        "hop": hop,
+        "direct": send_direct,
+        "pass": pass_on,
+        "cot": send_cots,
+        "grad": contract,
+    }
+    for step, *where in SCHEDULE:
+        run[step](*where)
+    weights()
     gsend[...] = grad[...].astype(BF16)
 
     def grad_copy(k):
@@ -271,17 +322,16 @@
             device_id_type=MESH,
         )
 
-    for k in (4, 3, 5, 2, 6, 1, 7):
-        grad_copy(k).start()
+    for k in REP_HOPS:
+        moving.start(("grad", k), grad_copy(k))
     own_rows = pl.ds(pl.multiple_of(r * OWN, OWN), OWN)
     gradient = grad[own_rows, :]
     loads[5].wait()
     loads[6].wait()
-    for k in range(1, 8):
-        grad_copy(k).wait_recv()
-    for k in range(1, 8):
+    for k in REP_HOPS:
+        moving.arrived(("grad", k))
+    for k in REP_HOPS:
         gradient += grecv[k].astype(F32)
-
     gradient_out[...] = gradient
     upd[own_rows, :] = adam(m1_v[...], m2_v[...], gradient)[2]
 
@@ -295,26 +345,10 @@
             device_id_type=MESH,
         )
 
-    for k in (4, 3, 5, 2, 6, 1, 7):
-        update_copy(k).start()
-    for copy in x_copies:
-        copy.wait_send()
-    for q in range(1, 16):
-        cot_copy(q).wait_send()
-        token_copy(q).wait_send()
-    for chunk in range(LAST):
-        for k in DIRECT:
-            direct(chunk, k).wait_send()
-        for copy in forwards(chunk):
-            copy.wait_send()
-    for k in range(1, 8):
-        direct(LAST, k).wait_send()
-        grad_copy(k).wait_send()
-    for k in range(1, 8):
-        update_copy(k).wait_recv()
+    for k in REP_HOPS:
+        moving.start(("update", k), update_copy(k))
+    moving.finish()
     update_out[...] = upd[...]
-    for k in range(1, 8):
-        update_copy(k).wait_send()
 
 
 def finish(gradient_ref, update_ref, basis_ref, m1_ref, m2_ref, m1_out, m2_out, delta_out):

time: 104 us -> 101 us (0.971)
  the two profiles are of different devices: /device:TPU:5 before, /device:TPU:128 now
where the time goes in v3:
time: 101 us
  Pallas kernels  100 us (99%)
    pallas_call x1, Pallas kernels, shards(): pl.pallas_call(kernel, out_shape=(jax.ShapeDtypeStruct((OWN, FEAT), F32),...  97.8 us
    pallas_call x1, Pallas kernels, shards(): pl.pallas_call(finish, out_shape=(jax.ShapeDtypeStruct((1, OWN, FEAT), F3...  2.4 us

profile of v3, /device:TPU:128, one launch (start us, length us, event | category | flops | bytes accessed | tf_op | source)
XLA Modules:
  0.0 100.8 jit_solution(7167496751619816142)
XLA Ops:
  0.6 97.8 %shard_map.103 = (f32[64,256]{1,0:T(8,128)}, bf16[512,256]{1,0:T(8,128)(2,1)}) custom-call(s32[8,8,16]{2,1,0:T(8,128)} %bitcast.5, bf16[8,8,16,256]{3,2,1,0:T(8,128)(2,1)} %bitcast.3, bf16[8,8,16,256]{3,2,1,0:T(8,128)(2,1)} %bitcast.4, bf16[1,2048,768]{2,1,0:T(8,128)(2,1)} %gate_hbm.1, bf16[1,2048,768]{2,1,0:T(8,128)(2,1)} %up_hbm.1, ...), custom_call_target="tpu_custom_call" | custom-call | tf_op jit(solution)/shard_map/pallas_call | solution.py:376
  98.4 2.4 %shard_map.104 = (f32[1,64,256]{2,1,0:T(8,128)}, f32[1,64,256]{2,1,0:T(8,128)}, bf16[1,768,256]{2,1,0:T(8,128)(2,1)}) custom-call(f32[64,256]{1,0:T(8,128)} %get-tuple-element.5.gradient_ref, bf16[512,256]{1,0:T(8,128)(2,1)} %get-tuple-element.6.update_ref, bf16[1,768,512]{2,1,0:T(8,128)(2,1)} %basis_ref.1, f32[1,64,256]{2,1,0:T(8,128)} %m1_ref.1, ...), custom_call_target="tpu_custom_call" | custom-call | flops 201326592 | bytes 2097152 | tf_op jit(solution)/shard_map/pallas_call | solution.py:423

commit v4 on v3

--- a/solution.py
+++ b/solution.py
@@ -23,6 +23,8 @@
 MODEL = 2048
 FF = 768
 OWN = 64
+PARTS = 2
+PART = OWN // PARTS
 
 SLOTS = (
     (0, 0), (0, 1), (1, 0), (1, 1), (-1, 0), (-1, 1),
@@ -39,8 +41,8 @@
 REP_HOPS = (4, 3, 5, 2, 6, 1, 7)
 SCHEDULE = (
     ("tokens", 0), ("tokens", 1),
-    ("project", 0), ("hop", 0, 0), ("tokens", 2),
-    ("project", 1), ("hop", 1, 0), ("hop", 0, 1), ("tokens", 3), ("hop", 0, 2), ("hop", 1, 1),
+    ("project", 0), ("hop", 0, 0), ("tokens", 2), ("hop", 0, 1),
+    ("project", 1), ("hop", 1, 0), ("tokens", 3), ("hop", 0, 2), ("hop", 1, 1),
     ("project", 2), ("direct", 2), ("hop", 0, 3), ("hop", 1, 2),
     ("project", 3), ("direct", 3), ("cot",), ("hop", 1, 3), ("pass", 2), ("pass", 3),
     ("grad", 0), ("grad", 1), ("grad", 2), ("grad", 3),
@@ -311,42 +313,47 @@
     weights()
     gsend[...] = grad[...].astype(BF16)
 
-    def grad_copy(k):
-        rows = pl.ds(pl.multiple_of(turn(r, k) * OWN, OWN), OWN)
-        return pltpu.make_async_remote_copy(
-            src_ref=gsend.at[rows],
-            dst_ref=grecv.at[k],
-            send_sem=gs.at[k],
-            recv_sem=gr.at[k],
+    def part_rows(owner, part):
+        return pl.ds(pl.multiple_of(owner * OWN + part * PART, PART), PART)
+
+    def grad_copy(k, part):
+        return pltpu.make_async_remote_copy(
+            src_ref=gsend.at[part_rows(turn(r, k), part)],
+            dst_ref=grecv.at[k, pl.ds(part * PART, PART)],
+            send_sem=gs.at[part, k],
+            recv_sem=gr.at[part, k],
             device_id={"rep": turn(r, k)},
             device_id_type=MESH,
         )
 
-    for k in REP_HOPS:
-        moving.start(("grad", k), grad_copy(k))
-    own_rows = pl.ds(pl.multiple_of(r * OWN, OWN), OWN)
-    gradient = grad[own_rows, :]
+    def update_copy(k, part):
+        rows = part_rows(r, part)
+        return pltpu.make_async_remote_copy(
+            src_ref=upd.at[rows],
+            dst_ref=upd.at[rows],
+            send_sem=us.at[part, k],
+            recv_sem=ur.at[part, k],
+            device_id={"rep": turn(r, k)},
+            device_id_type=MESH,
+        )
+
+    for part in range(PARTS):
+        for k in REP_HOPS:
+            moving.start(("grad", k, part), grad_copy(k, part))
     loads[5].wait()
     loads[6].wait()
-    for k in REP_HOPS:
-        moving.arrived(("grad", k))
-    for k in REP_HOPS:
-        gradient += grecv[k].astype(F32)
-    gradient_out[...] = gradient
-    upd[own_rows, :] = adam(m1_v[...], m2_v[...], gradient)[2]
-
-    def update_copy(k):
-        return pltpu.make_async_remote_copy(
-            src_ref=upd.at[own_rows],
-            dst_ref=upd.at[own_rows],
-            send_sem=us.at[k],
-            recv_sem=ur.at[k],
-            device_id={"rep": turn(r, k)},
-            device_id_type=MESH,
-        )
-
-    for k in REP_HOPS:
-        moving.start(("update", k), update_copy(k))
+    for part in range(PARTS):
+        local = pl.ds(part * PART, PART)
+        rows = part_rows(r, part)
+        gradient = grad[rows, :]
+        for k in REP_HOPS:
+            moving.arrived(("grad", k, part))
+        for k in REP_HOPS:
+            gradient += grecv[k, local].astype(F32)
+        gradient_out[local, :] = gradient
+        upd[rows, :] = adam(m1_v[local, :], m2_v[local, :], gradient)[2]
+        for k in REP_HOPS:
+            moving.start(("update", k, part), update_copy(k, part))
     moving.finish()
     update_out[...] = upd[...]
 
@@ -404,8 +411,8 @@
             dma((16,)), dma((16,)),
             dma((16,)), dma((16,)),
             dma((len(CHUNKS), 8)), dma((len(CHUNKS), 8)),
-            dma((8,)), dma((8,)),
-            dma((8,)), dma((8,)),
+            dma((PARTS, 8)), dma((PARTS, 8)),
+            dma((PARTS, 8)), dma((PARTS, 8)),
         ],
         compiler_params=pltpu.CompilerParams(
             collective_id=0, has_side_effects=True, vmem_limit_bytes=63 * 1024 * 1024

time: 101 us -> 98.4 us (0.974)
  the two profiles are of different devices: /device:TPU:128 before, /device:TPU:2 now
where the time goes in v4:
time: 98.4 us; the launch traced here: 98.2 us
  Pallas kernels  97.5 us (99%)
    pallas_call x1, Pallas kernels, shards(): pl.pallas_call(kernel, out_shape=(jax.ShapeDtypeStruct((OWN, FEAT), F32),...  95.1 us
    pallas_call x1, Pallas kernels, shards(): pl.pallas_call(finish, out_shape=(jax.ShapeDtypeStruct((1, OWN, FEAT), F3...  2.4 us

profile of v4, /device:TPU:2, one launch (start us, length us, event | category | flops | bytes accessed | tf_op | source)
XLA Modules:
  0.0 98.2 jit_solution(13831394679487745766)
XLA Ops:
  0.6 95.1 %shard_map.103 = (f32[64,256]{1,0:T(8,128)}, bf16[512,256]{1,0:T(8,128)(2,1)}) custom-call(s32[8,8,16]{2,1,0:T(8,128)} %bitcast.5, bf16[8,8,16,256]{3,2,1,0:T(8,128)(2,1)} %bitcast.3, bf16[8,8,16,256]{3,2,1,0:T(8,128)(2,1)} %bitcast.4, bf16[1,2048,768]{2,1,0:T(8,128)(2,1)} %gate_hbm.1, bf16[1,2048,768]{2,1,0:T(8,128)(2,1)} %up_hbm.1, ...), custom_call_target="tpu_custom_call" | custom-call | tf_op jit(solution)/shard_map/pallas_call | solution.py:383
  95.8 2.4 %shard_map.104 = (f32[1,64,256]{2,1,0:T(8,128)}, f32[1,64,256]{2,1,0:T(8,128)}, bf16[1,768,256]{2,1,0:T(8,128)(2,1)}) custom-call(f32[64,256]{1,0:T(8,128)} %get-tuple-element.5.gradient_ref, bf16[512,256]{1,0:T(8,128)(2,1)} %get-tuple-element.6.update_ref, bf16[1,768,512]{2,1,0:T(8,128)(2,1)} %basis_ref.1, f32[1,64,256]{2,1,0:T(8,128)} %m1_ref.1, ...), custom_call_target="tpu_custom_call" | custom-call | flops 201326592 | bytes 2097152 | tf_op jit(solution)/shard_map/pallas_call | solution.py:430

commit v5 on v4

--- a/solution.py
+++ b/solution.py
@@ -23,7 +23,7 @@
 MODEL = 2048
 FF = 768
 OWN = 64
-PARTS = 2
+PARTS = 4
 PART = OWN // PARTS
 
 SLOTS = (

time: 98.4 us -> 99.4 us (1.010)
  Pallas kernels: 97.5 us -> 98.5 us
where the time goes in v5:
time: 99.4 us; the launch traced here: 99.1 us
  Pallas kernels  98.5 us (99%)
    pallas_call x1, Pallas kernels, shards(): pl.pallas_call(kernel, out_shape=(jax.ShapeDtypeStruct((OWN, FEAT), F32),...  96.1 us
    pallas_call x1, Pallas kernels, shards(): pl.pallas_call(finish, out_shape=(jax.ShapeDtypeStruct((1, OWN, FEAT), F3...  2.41 us

profile of v5, /device:TPU:2, one launch (start us, length us, event | category | flops | bytes accessed | tf_op | source)
XLA Modules:
  0.0 99.1 jit_solution(12979910307709259724)
XLA Ops:
  0.6 96.1 %shard_map.103 = (f32[64,256]{1,0:T(8,128)}, bf16[512,256]{1,0:T(8,128)(2,1)}) custom-call(s32[8,8,16]{2,1,0:T(8,128)} %bitcast.5, bf16[8,8,16,256]{3,2,1,0:T(8,128)(2,1)} %bitcast.3, bf16[8,8,16,256]{3,2,1,0:T(8,128)(2,1)} %bitcast.4, bf16[1,2048,768]{2,1,0:T(8,128)(2,1)} %gate_hbm.1, bf16[1,2048,768]{2,1,0:T(8,128)(2,1)} %up_hbm.1, ...), custom_call_target="tpu_custom_call" | custom-call | tf_op jit(solution)/shard_map/pallas_call | solution.py:383
  96.7 2.4 %shard_map.104 = (f32[1,64,256]{2,1,0:T(8,128)}, f32[1,64,256]{2,1,0:T(8,128)}, bf16[1,768,256]{2,1,0:T(8,128)(2,1)}) custom-call(f32[64,256]{1,0:T(8,128)} %get-tuple-element.5.gradient_ref, bf16[512,256]{1,0:T(8,128)(2,1)} %get-tuple-element.6.update_ref, bf16[1,768,512]{2,1,0:T(8,128)(2,1)} %basis_ref.1, f32[1,64,256]{2,1,0:T(8,128)} %m1_ref.1, ...), custom_call_target="tpu_custom_call" | custom-call | flops 201326592 | bytes 2097152 | tf_op jit(solution)/shard_map/pallas_call | solution.py:430
